TPU v7x, 256 devices: a whole 4x4x8 slice. The times are simulated.
256 devices in a mesh: blk: 16 (over y_hi, z), frames: 16 (over x, y_lo, core).
Axes of the slice: x: 4, y: 4 (y_hi: 2, y_lo: 2; y = y_hi * 2 + y_lo), z: 8, core: 2. Of those that a mesh axis runs over, the one named last changes fastest.
Arguments:
- coarse_query: bfloat16 [512, 16, 256], P('blk'), may hold values from -125 to 125
- coarse_feat: bfloat16 [64, 8160, 256], P('frames', 'blk'), may hold values from -61 to 61
- fine_query: bfloat16 [512, 128], P(('blk', 'frames')), may hold values from -175 to 175
- fine_tiles: bfloat16 [64, 1024, 64, 128], P('frames', 'blk'), may hold values from -61 to 61
- track_pos: int32 [2, 64, 512], P(None, None, ('blk', 'frames')), may hold values from 0 to 959, as said below
- tile_list: int32 [64, 16, 16, 8], P('frames', 'blk'), may hold values from 0 to 63, as said below
- tile_valid: int32 [64, 16, 16, 8], P('frames', 'blk'), may hold values from 0 to 1, as said below
Outputs:
- coarse_pos: float32 [2, 64, 512], P(None, 'frames', 'blk')
- fine_offset: float32 [2, 64, 512], P(None, None, ('blk', 'frames'))
Inputs may be any that keep to these rules, and one draw needn't show every extreme that they name: `tile_list`: in each list the valid slots come first and name distinct tiles of the group's window; padded slots hold 63; in every frame and group some owner's list is full. `tile_valid`: each list has at least 4 valid slots. `track_pos`: rows lie below 544 and columns below 960.
All inputs are finite; a program needn't handle non-finite values.
Results may differ from a plain program's by a relative error of at most 0.0003.
Values may be sent and summed in bfloat16 or wider, within the bound.
A program may use at most 192 MiB of HBM per device.

v0:
```python
import math
import jax
import jax.numpy as jnp
from jax import lax
from jax.sharding import PartitionSpec as P

GH = 68
GW = 120
TILE = 8
spread_cells = 32.0


def refine_frame(descriptors, tile_block, tile_ids, tile_live, track_row, track_col, base_cell):
    slot_count, cell_count, channels = tile_block.shape
    flat_tiles = tile_block.reshape(slot_count * cell_count, channels)
    scores = jnp.einsum(
        "nc,kc->nk", descriptors, flat_tiles, preferred_element_type=jnp.float32
    ) * (1.0 / math.sqrt(channels))
    global_cell = base_cell + tile_ids
    inner_cell = jnp.arange(cell_count, dtype=jnp.int32)
    cell_row = (global_cell // GW * TILE)[:, None] + (inner_cell // TILE)[None, :]
    cell_col = (global_cell % GW * TILE)[:, None] + (inner_cell % TILE)[None, :]
    cell_row = cell_row.reshape(-1).astype(jnp.float32)
    cell_col = cell_col.reshape(-1).astype(jnp.float32)
    distance = (cell_row[None, :] - track_row[:, None]) ** 2 + (
        cell_col[None, :] - track_col[:, None]
    ) ** 2
    scores = scores - distance * (0.5 / (spread_cells * spread_cells))
    live_cells = jnp.broadcast_to(tile_live[:, None] > 0, (slot_count, cell_count)).reshape(-1)
    scores = jnp.where(live_cells[None, :], scores, -1e30)
    highest = jnp.max(scores, axis=1, keepdims=True)
    weights = jnp.exp(scores - highest)
    totals = jnp.sum(weights, axis=1)
    mean_row = jnp.sum(weights * cell_row[None, :], axis=1) / totals
    mean_col = jnp.sum(weights * cell_col[None, :], axis=1) / totals
    return ((mean_row - track_row) / spread_cells, (mean_col - track_col) / spread_cells)


def coarse_finish(row_mean, col_mean):
    row_heads = jnp.mean(row_mean, axis=2)
    col_heads = jnp.mean(col_mean, axis=2)
    return jnp.stack(
        [(row_heads - (GH - 1) / 2.0) / (GH / 4.0), (col_heads - (GW - 1) / 2.0) / (GW / 4.0)]
    )


def body(coarse_query, coarse_feat, fine_query, fine_tiles, track_pos, tile_list, tile_valid):
    track_group, heads, channels = coarse_query.shape
    frames_here, region, _ = coarse_feat.shape
    scale = 1.0 / math.sqrt(channels)
    group_start = lax.axis_index("blk") * region
    query_rows = coarse_query.reshape(track_group * heads, channels)
    row_count = query_rows.shape[0]
    zeros_state = jnp.zeros((frames_here, row_count), jnp.float32)
    shard_piece = lax.all_gather(coarse_feat, "blk", axis=1, tiled=True)
    first_pos = jnp.int32(0)
    maxima = jnp.full((frames_here, row_count), -jnp.inf, jnp.float32)
    totals = zeros_state
    row_sums = zeros_state
    col_sums = zeros_state
    length = shard_piece.shape[1]
    for offset in range(0, length, 512):
        feat_block = shard_piece[:, offset : offset + 512]
        scores = (
            jnp.einsum("rc,fpc->frp", query_rows, feat_block, preferred_element_type=jnp.float32)
            * scale
        )
        positions = first_pos + offset + jnp.arange(feat_block.shape[1], dtype=jnp.int32)
        pos_row = (positions // GW).astype(jnp.float32)
        pos_col = (positions % GW).astype(jnp.float32)
        new_max = jnp.maximum(maxima, jnp.max(scores, axis=2))
        retain = jnp.exp(maxima - new_max)
        weights = jnp.exp(scores - new_max[:, :, None])
        totals = totals * retain + jnp.sum(weights, axis=2)
        row_sums = row_sums * retain + jnp.sum(weights * pos_row[None, None, :], axis=2)
        col_sums = col_sums * retain + jnp.sum(weights * pos_col[None, None, :], axis=2)
        maxima = new_max
    final_state = (maxima, totals, row_sums, col_sums)
    row_mean = (final_state[2] / final_state[1]).reshape(frames_here, track_group, heads)
    col_mean = (final_state[3] / final_state[1]).reshape(frames_here, track_group, heads)
    coarse_pos = coarse_finish(row_mean, col_mean)
    list_ids = jnp.transpose(tile_list[:, 0], (1, 0, 2))
    list_live = jnp.transpose(tile_valid[:, 0], (1, 0, 2))
    picked = fine_tiles[jnp.arange(frames_here, dtype=jnp.int32)[None, :, None], list_ids]
    per_frame = jax.vmap(refine_frame, in_axes=(None, 0, 0, 0, 0, 0, None))
    got_tiles, got_ids, got_live = (
        lax.all_to_all(picked, "frames", split_axis=0, concat_axis=0, tiled=True),
        lax.all_to_all(list_ids, "frames", split_axis=0, concat_axis=0, tiled=True),
        lax.all_to_all(list_live, "frames", split_axis=0, concat_axis=0, tiled=True),
    )
    window = got_tiles.shape[0] * got_tiles.shape[1]
    got_tiles = got_tiles.reshape((window,) + got_tiles.shape[2:])
    got_ids = got_ids.reshape(window, -1)
    got_live = got_live.reshape(window, -1)
    places = track_pos.astype(jnp.float32)
    rows_out, cols_out = per_frame(
        fine_query, got_tiles, got_ids, got_live, places[0], places[1], group_start
    )
    fine_offset = jnp.stack([rows_out, cols_out])
    return (coarse_pos, fine_offset)


def solution(mesh):
    return jax.shard_map(
        body,
        mesh=mesh,
        in_specs=(
            P("blk", None, None),
            P("frames", "blk", None),
            P(("blk", "frames"), None),
            P("frames", "blk", None, None),
            P(None, None, ("blk", "frames")),
            P("frames", "blk", None, None),
            P("frames", "blk", None, None),
        ),
        out_specs=(P(None, "frames", "blk"), P(None, None, ("blk", "frames"))),
        check_vma=False,
    )
```

profile of v0, /device:TPU:1, one launch (start us, length us, event | category | flops | bytes accessed | tf_op | source)
XLA Modules:
  0.0 419.7 jit_solution(9521634388056625112)
XLA Ops:
  9.3 6.8 %all-to-all-start.2 = ((s32[16,4,8]{2,1,0:T(4,128)}), s32[16,4,8]{2,1,0:T(4,128)S(1)}, u32[]{:S(2)}, u32[]{:S(2)}) async-start(s32[16,4,8]{2,1,0:T(4,128)} %bitcast.25), calls=%async_computation.2 | async-start | bytes 65536 | tf_op jit(solution)/shard_map/all_to_all | solution.py:88
  17.5 4.4 %all-to-all-done.2 = s32[16,4,8]{2,1,0:T(4,128)S(1)} async-done(((s32[16,4,8]{2,1,0:T(4,128)}), s32[16,4,8]{2,1,0:T(4,128)S(1)}, u32[]{:S(2)}, u32[]{:S(2)}) %all-to-all-start.2) | async-done | bytes 2080 | tf_op jit(solution)/shard_map/all_to_all | solution.py:88
  22.0 3.7 all-to-all-start
  26.5 10.3 %gather_fusion = bf16[512,64,128]{2,1,0:T(8,128)(2,1)} fusion(bf16[4,64,64,128]{3,2,1,0:T(8,128)(2,1)} %param.10, s32[512]{0:T(512)S(1)} %reshape.890), kind=kCustom, calls=%fused_computation | custom fusion | bytes 16781312 | tf_op jit(solution)/shard_map/gather | solution.py:84
  36.8 5.9 %all-to-all-start.1 = ((bf16[16,4,8,64,128]{4,3,2,1,0:T(8,128)(2,1)}), bf16[16,4,8,64,128]{4,3,2,1,0:T(8,128)(2,1)}, u32[]{:S(2)}, u32[]{:S(2)}) async-start(bf16[16,4,8,64,128]{4,3,2,1,0:T(8,128)(2,1)} %bitcast.260), calls=%async_computation.1 | async-start | bytes 16777216 | tf_op jit(solution)/shard_map/all_to_all | solution.py:87
  44.4 129.9 %all-to-all-done.1 = bf16[16,4,8,64,128]{4,3,2,1,0:T(8,128)(2,1)} async-done(((bf16[16,4,8,64,128]{4,3,2,1,0:T(8,128)(2,1)}), bf16[16,4,8,64,128]{4,3,2,1,0:T(8,128)(2,1)}, u32[]{:S(2)}, u32[]{:S(2)}) %all-to-all-start.1) | async-done | bytes 8388640 | tf_op jit(solution)/shard_map/all_to_all | solution.py:87
  174.3 5.8 %multiply_reduce_fusion.33 = (f32[64,2]{1,0:T(8,128)S(1)}, f32[64,2]{1,0:T(8,128)S(1)}, f32[64,2]{1,0:T(8,128)S(1)}) fusion(f32[64,512]{1,0:T(8,128)S(1)} %get-tuple-element.151, f32[64,512]{1,0:T(8,128)S(1)} %get-tuple-element.150, bf16[64,512,128]{2,1,0:T(8,128)(2,1)} %bitcast.29, pred[64,512]{1,0:T(8,128)(4,1)S(1)} %broadcast_in_dim.23, ...), kind=kOutput, calls=%fused_computation.137 | convolution fusion | flops 17760512 | bytes 8686592 | tf_op jit(solution)/shard_map/vmap()/sub | solution.py:32
  180.9 113.8 %all-gather.2.cloned.1.call-done = bf16[4,8160,256]{2,0,1:T(4,128)(2,1)} async-done(((bf16[4,510,256]{2,0,1:T(4,128)(2,1)}), bf16[4,8160,256]{2,0,1:T(4,128)(2,1)}) %all-gather.2.cloned.1.call-update) | async-done | bytes 16711696 | tf_op jit(solution)/shard_map/all_gather | solution.py:55
  298.8 10.4 %fusion.197 = (bf16[4,512,256]{2,0,1:T(4,128)(2,1)S(1)}, bf16[4,512,256]{2,0,1:T(4,128)(2,1)S(1)}, bf16[4,512,256]{2,0,1:T(4,128)(2,1)S(1)}, bf16[4,512,256]{2,0...) fusion(bf16[4,8160,256]{2,0,1:T(4,128)(2,1)} %all-gather.2.clon, ...), kind=kLoop, calls=%fused_computation.377 | loop fusion | bytes 31457280 | tf_op jit(solution)/shard_map/slice | solution.py:63
  309.2 2.7 bitcast_reduce_fusion
  311.9 2.7 bitcast_reduce_fusion.1
  320.0 2.7 bitcast_reduce_fusion.4
  322.8 2.7 bitcast_reduce_fusion.5
  328.2 2.8 bitcast_reduce_fusion.7
  339.0 2.8 bitcast_reduce_fusion.11
  351.4 3.8 multiply_reduce_fusion.31
  355.3 6.8 %multiply_reduce_fusion.15 = (f32[4,512]{1,0:T(4,128)S(1)}, f32[4,512]{1,0:T(4,128)S(1)}, f32[4,512]{1,0:T(4,128)S(1)}, f32[4,512]{1,0:T(4,128)S(1)}, f32[4,512]{1,0:T(4,128)S(1)}, /*index=5*/f32[4,512]{1,0:T(4,128)S(1)}) fusion(f32[4,512,512]{2,1,0:T(8,128)} %get-tuple-element.96, f32[512]{0:T(512)S(1)} %fusion.108, f32[4,512]{1,0:T(4,128)S(1)} %get-tuple-element.54, ...), kind=kLoop, calls=%fused_computation.62 | loop fusion | flops 14667776 | bytes 8462336 | tf_op jit(solution)/shard_map/reduce_sum | solution.py:75
  362.3 6.8 %multiply_reduce_fusion.17 = (f32[4,512]{1,0:T(4,128)S(1)}, f32[4,512]{1,0:T(4,128)S(1)}, f32[4,512]{1,0:T(4,128)S(1)}, f32[4,512]{1,0:T(4,128)S(1)}, f32[4,512]{1,0:T(4,128)S(1)}, /*index=5*/f32[4,512]{1,0:T(4,128)S(1)}) fusion(f32[4,512,512]{2,1,0:T(8,128)} %get-tuple-element.100, f32[512]{0:T(512)S(1)} %fusion.116, f32[4,512]{1,0:T(4,128)S(1)} %get-tuple-element.56, ...), kind=kLoop, calls=%fused_computation.64 | loop fusion | flops 14667776 | bytes 8462336 | tf_op jit(solution)/shard_map/reduce_sum | solution.py:75
  369.2 6.8 %multiply_reduce_fusion.19 = (f32[4,512]{1,0:T(4,128)S(1)}, f32[4,512]{1,0:T(4,128)S(1)}, f32[4,512]{1,0:T(4,128)S(1)}, f32[4,512]{1,0:T(4,128)S(1)}, f32[4,512]{1,0:T(4,128)S(1)}, /*index=5*/f32[4,512]{1,0:T(4,128)S(1)}) fusion(f32[4,512,512]{2,1,0:T(8,128)} %get-tuple-element.104, f32[512]{0:T(512)S(1)} %fusion.124, f32[4,512]{1,0:T(4,128)S(1)} %get-tuple-element.58, ...), kind=kLoop, calls=%fused_computation.66 | loop fusion | flops 14667776 | bytes 8462336 | tf_op jit(solution)/shard_map/reduce_sum | solution.py:75
  376.2 6.8 %multiply_reduce_fusion.21 = (f32[4,512]{1,0:T(4,128)S(1)}, f32[4,512]{1,0:T(4,128)S(1)}, f32[4,512]{1,0:T(4,128)S(1)}, f32[4,512]{1,0:T(4,128)S(1)}, f32[4,512]{1,0:T(4,128)S(1)}, /*index=5*/f32[4,512]{1,0:T(4,128)S(1)}) fusion(f32[4,512,512]{2,1,0:T(8,128)} %get-tuple-element.108, f32[512]{0:T(512)S(1)} %fusion.132, f32[4,512]{1,0:T(4,128)S(1)} %get-tuple-element.60, ...), kind=kLoop, calls=%fused_computation.68 | loop fusion | flops 14667776 | bytes 8462336 | tf_op jit(solution)/shard_map/reduce_sum | solution.py:75
  383.2 7.0 %multiply_reduce_fusion.23 = (f32[4,512]{1,0:T(4,128)S(1)}, f32[4,512]{1,0:T(4,128)S(1)}, f32[4,512]{1,0:T(4,128)S(1)}, f32[4,512]{1,0:T(4,128)S(1)}, f32[4,512]{1,0:T(4,128)S(1)}, /*index=5*/f32[4,512]{1,0:T(4,128)S(1)}) fusion(f32[4,512,512]{2,1,0:T(8,128)} %get-tuple-element.112, f32[512]{0:T(512)S(1)} %fusion.140, f32[4,512]{1,0:T(4,128)S(1)} %get-tuple-element.62, ...), kind=kLoop, calls=%fused_computation.70 | loop fusion | flops 14667776 | bytes 8462336 | tf_op jit(solution)/shard_map/reduce_sum | solution.py:75
  390.3 6.8 %multiply_reduce_fusion.25 = (f32[4,512]{1,0:T(4,128)S(1)}, f32[4,512]{1,0:T(4,128)S(1)}, f32[4,512]{1,0:T(4,128)S(1)}, f32[4,512]{1,0:T(4,128)S(1)}, f32[4,512]{1,0:T(4,128)S(1)}, /*index=5*/f32[4,512]{1,0:T(4,128)S(1)}) fusion(f32[4,512,512]{2,1,0:T(8,128)} %get-tuple-element.116, f32[512]{0:T(512)S(1)} %fusion.148, f32[4,512]{1,0:T(4,128)S(1)} %get-tuple-element.64, ...), kind=kLoop, calls=%fused_computation.72 | loop fusion | flops 14667776 | bytes 8462336 | tf_op jit(solution)/shard_map/reduce_sum | solution.py:75
  397.3 6.8 %multiply_reduce_fusion.27 = (f32[4,512]{1,0:T(4,128)S(1)}, f32[4,512]{1,0:T(4,128)S(1)}, f32[4,512]{1,0:T(4,128)S(1)}, f32[4,512]{1,0:T(4,128)S(1)}, f32[4,512]{1,0:T(4,128)S(1)}, /*index=5*/f32[4,512]{1,0:T(4,128)S(1)}) fusion(f32[4,512,512]{2,1,0:T(8,128)} %get-tuple-element.120, f32[512]{0:T(512)S(1)} %fusion.156, f32[4,512]{1,0:T(4,128)S(1)} %get-tuple-element.66, ...), kind=kLoop, calls=%fused_computation.74 | loop fusion | flops 14667776 | bytes 8462336 | tf_op jit(solution)/shard_map/reduce_sum | solution.py:75
  404.2 3.8 multiply_reduce_fusion.29
  (150 shorter events, 42.0 us)
Async XLA Ops:
  7.2 289.1 %copy-start = (bf16[32,16,256]{2,1,0:T(8,128)(2,1)S(1)}, bf16[32,16,256]{2,1,0:T(8,128)(2,1)}, u32[]{:S(2)}) copy-start(bf16[32,16,256]{2,1,0:T(8,128)(2,1)} %param.7) | copy-start | bytes 786436
  7.2 287.5 %all-gather.2.cloned.1.call-start = ((), (), s32[]{:S(2)}) async-start(), calls=%async_computation.3 | async-start | bytes 17756160 | tf_op jit(solution)/shard_map/all_gather | solution.py:55
  9.3 12.7 %all-to-all-start.2 = ((s32[16,4,8]{2,1,0:T(4,128)}), s32[16,4,8]{2,1,0:T(4,128)S(1)}, u32[]{:S(2)}, u32[]{:S(2)}) async-start(s32[16,4,8]{2,1,0:T(4,128)} %bitcast.25), calls=%async_computation.2 | async-start | bytes 65536 | tf_op jit(solution)/shard_map/all_to_all | solution.py:88
  22.0 14.8 %all-to-all-start = ((s32[16,4,8]{2,1,0:T(4,128)}), s32[16,4,8]{2,1,0:T(4,128)S(1)}, u32[]{:S(2)}, u32[]{:S(2)}) async-start(s32[16,4,8]{2,1,0:T(4,128)} %bitcast.22), calls=%async_computation | async-start | bytes 65536 | tf_op jit(solution)/shard_map/all_to_all | solution.py:89
  36.8 6.1 %copy-start.1 = (s32[2,64,2]{1,2,0:T(2,128)S(1)}, s32[2,64,2]{1,2,0:T(2,128)}, u32[]{:S(2)}) copy-start(s32[2,64,2]{1,2,0:T(2,128)} %param.11) | copy-start | bytes 3076
  36.8 137.5 %copy-start.2 = (bf16[2,128]{1,0:T(2,128)(2,1)S(1)}, bf16[2,128]{1,0:T(2,128)(2,1)}, u32[]{:S(2)}) copy-start(bf16[2,128]{1,0:T(2,128)(2,1)} %param.9) | copy-start | bytes 1540
  36.8 137.5 %all-to-all-start.1 = ((bf16[16,4,8,64,128]{4,3,2,1,0:T(8,128)(2,1)}), bf16[16,4,8,64,128]{4,3,2,1,0:T(8,128)(2,1)}, u32[]{:S(2)}, u32[]{:S(2)}) async-start(bf16[16,4,8,64,128]{4,3,2,1,0:T(8,128)(2,1)} %bitcast.260), calls=%async_computation.1 | async-start | bytes 16777216 | tf_op jit(solution)/shard_map/all_to_all | solution.py:87
Sparse Core Ops, SparseCore 0:
  10.7 283.9 all-gather.1
where the time goes:
time: 426 us; the launch traced here: 420 us
  waiting for transfers between devices  249 us (58%)
  other arithmetic  58.7 us (14%)
  matrix products  49.1 us (12%)
  local copies, waits for them, and re-layouts  31.7 us (7%)
  starting transfers between devices  16.4 us (4%)
  between operations  15 us (4%)
    all_to_all x1, waiting for transfers between devices, body(): lax.all_to_all(picked, 'frames', split_axis=0, concat_axis=0, tiled=True)  130 us
    all_gather x1, waiting for transfers between devices, body(): shard_piece = lax.all_gather(coarse_feat, 'blk', axis=1, tiled=True)  114 us
    reduce_sum x9, other arithmetic, body(): jnp.sum(weights * pos_row[None, None, :], axis=2)  55.3 us
    dot_general x16, matrix products, body(): jnp.einsum('rc,fpc->frp', query_rows, feat_block, preferred_element_type=...  43.3 us
    slice x2, local copies, waits for them, and re-layouts, body(): feat_block = shard_piece[:, offset:offset + 512]  11.9 us
    gather x1, local copies, waits for them, and re-layouts, body(): fine_tiles[jnp.arange(frames_here, dtype=jnp.int32)[None, :, None], list_...  10.3 us
  transfers between devices with their start and end apart: 4, of which 3 were waited for; matrix products, arithmetic and copies ran while one was open for 5% of the time, Pallas kernels for 0%

commit v1 on v0

--- a/solution.py
+++ b/solution.py
@@ -52,7 +52,8 @@
     query_rows = coarse_query.reshape(track_group * heads, channels)
     row_count = query_rows.shape[0]
     zeros_state = jnp.zeros((frames_here, row_count), jnp.float32)
-    shard_piece = lax.all_gather(coarse_feat, "blk", axis=1, tiled=True)
+    stack = jnp.stack([coarse_feat] * lax.axis_size("blk"))
+    shard_piece = jnp.concatenate(lax.all_to_all(stack, "blk", 0, 0), axis=1)
     first_pos = jnp.int32(0)
     maxima = jnp.full((frames_here, row_count), -jnp.inf, jnp.float32)
     totals = zeros_state

time: 426 us -> 651 us (1.53)
  the two profiles are of different devices: /device:TPU:1 before, /device:TPU:131 now
where the time goes in v1:
time: 651 us; the launch traced here: 645 us
  waiting for transfers between devices  378 us (58%)
  blocking collectives  98.7 us (15%)
  other arithmetic  58.7 us (9%)
  matrix products  49.1 us (8%)
  local copies, waits for them, and re-layouts  39 us (6%)
  starting transfers between devices  20.1 us (3%)
    all_to_all x1, waiting for transfers between devices, body(): shard_piece = jnp.concatenate(lax.all_to_all(stack, 'blk', 0, 0), axis=1)  374 us
    all_to_all x1, blocking collectives, body(): lax.all_to_all(picked, 'frames', split_axis=0, concat_axis=0, tiled=True)  98.7 us
    reduce_sum x9, other arithmetic, body(): jnp.sum(weights * pos_row[None, None, :], axis=2)  55.3 us
    dot_general x16, matrix products, body(): jnp.einsum('rc,fpc->frp', query_rows, feat_block, preferred_element_type=...  43.3 us
  transfers between devices with their start and end apart: 3, of which 2 were waited for; matrix products, arithmetic and copies ran while one was open for 3% of the time, Pallas kernels for 0%

profile of v1, /device:TPU:131, one launch (start us, length us, event | category | flops | bytes accessed | tf_op | source)
XLA Modules:
  0.0 644.8 jit_solution(7219744034755076218)
XLA Ops:
  2.1 6.2 all-to-all-start.3
  9.6 3.3 all-to-all-done.3
  13.0 4.8 all-to-all-start.1
  18.6 9.8 %gather_fusion = bf16[512,64,128]{2,1,0:T(8,128)(2,1)} fusion(bf16[4,64,64,128]{3,2,1,0:T(8,128)(2,1)} %param.10, s32[512]{0:T(512)S(1)} %reshape.900), kind=kCustom, calls=%fused_computation | custom fusion | bytes 16781312 | tf_op jit(solution)/shard_map/gather | solution.py:85
  28.5 98.7 %all_to_all.20 = bf16[16,4,8,64,128]{4,3,2,1,0:T(8,128)(2,1)} all-to-all(bf16[16,4,8,64,128]{4,3,2,1,0:T(8,128)(2,1)} %bitcast.263), channel_id=1, replica_groups=mesh['blk'=16,'frames'=16] {'frames'}, dimensions={0} | all-to-all | bytes 16777216 | tf_op jit(solution)/shard_map/all_to_all | solution.py:88
  127.2 7.7 %stack.6 = bf16[16,4,510,256]{3,1,2,0:T(4,128)(2,1)} broadcast(bf16[4,510,256]{2,0,1:T(4,128)(2,1)S(1)} %copy-done.1), dimensions={1,2,3} | broadcast | bytes 17756160 | tf_op jit(solution)/shard_map/stack | solution.py:55
  134.9 9.1 %all-to-all-start = ((bf16[16,4,510,256]{3,1,2,0:T(4,128)(2,1)}), bf16[16,4,510,256]{3,1,2,0:T(4,128)(2,1)}, u32[]{:S(2)}, u32[]{:S(2)}) async-start(bf16[16,4,510,256]{3,1,2,0:T(4,128)(2,1)} %stack.6), calls=%async_computation | async-start | bytes 33423360 | tf_op jit(solution)/shard_map/all_to_all | solution.py:56
  145.8 5.8 multiply_reduce_fusion.33
  152.4 374.2 %all-to-all-done = bf16[16,4,510,256]{3,1,2,0:T(4,128)(2,1)} async-done(((bf16[16,4,510,256]{3,1,2,0:T(4,128)(2,1)}), bf16[16,4,510,256]{3,1,2,0:T(4,128)(2,1)}, u32[]{:S(2)}, u32[]{:S(2)}) %all-to-all-start) | async-done | bytes 16711712 | tf_op jit(solution)/shard_map/all_to_all | solution.py:56
  528.2 10.4 %fusion.197 = (bf16[4,512,256]{2,0,1:T(4,128)(2,1)S(1)}, bf16[4,512,256]{2,0,1:T(4,128)(2,1)S(1)}, bf16[4,512,256]{2,0,1:T(4,128)(2,1)S(1)}, bf16[4,512,256]{2,0...) fusion(bf16[4,8160,256]{2,0,1:T(4,128)(2,1)} %bitcast.1), kind=kLoop, calls=%fused_computation.377 | loop fusion | bytes 31457280 | tf_op jit(solution)/shard_map/slice | solution.py:64
  541.2 2.7 bitcast_reduce_fusion
  543.9 2.7 bitcast_reduce_fusion.1
  554.7 2.7 bitcast_reduce_fusion.5
  560.2 2.8 bitcast_reduce_fusion.7
  571.0 2.8 bitcast_reduce_fusion.11
  583.4 3.8 multiply_reduce_fusion.31
  587.3 6.8 %multiply_reduce_fusion.15 = (f32[4,512]{1,0:T(4,128)S(1)}, f32[4,512]{1,0:T(4,128)S(1)}, f32[4,512]{1,0:T(4,128)S(1)}, f32[4,512]{1,0:T(4,128)S(1)}, f32[4,512]{1,0:T(4,128)S(1)}, /*index=5*/f32[4,512]{1,0:T(4,128)S(1)}) fusion(f32[4,512,512]{2,1,0:T(8,128)} %get-tuple-element.96, f32[512]{0:T(512)S(1)} %fusion.108, f32[4,512]{1,0:T(4,128)S(1)} %get-tuple-element.54, ...), kind=kLoop, calls=%fused_computation.62 | loop fusion | flops 14667776 | bytes 8462336 | tf_op jit(solution)/shard_map/reduce_sum | solution.py:76
  594.2 6.8 %multiply_reduce_fusion.17 = (f32[4,512]{1,0:T(4,128)S(1)}, f32[4,512]{1,0:T(4,128)S(1)}, f32[4,512]{1,0:T(4,128)S(1)}, f32[4,512]{1,0:T(4,128)S(1)}, f32[4,512]{1,0:T(4,128)S(1)}, /*index=5*/f32[4,512]{1,0:T(4,128)S(1)}) fusion(f32[4,512,512]{2,1,0:T(8,128)} %get-tuple-element.100, f32[512]{0:T(512)S(1)} %fusion.116, f32[4,512]{1,0:T(4,128)S(1)} %get-tuple-element.56, ...), kind=kLoop, calls=%fused_computation.64 | loop fusion | flops 14667776 | bytes 8462336 | tf_op jit(solution)/shard_map/reduce_sum | solution.py:76
  601.2 6.8 %multiply_reduce_fusion.19 = (f32[4,512]{1,0:T(4,128)S(1)}, f32[4,512]{1,0:T(4,128)S(1)}, f32[4,512]{1,0:T(4,128)S(1)}, f32[4,512]{1,0:T(4,128)S(1)}, f32[4,512]{1,0:T(4,128)S(1)}, /*index=5*/f32[4,512]{1,0:T(4,128)S(1)}) fusion(f32[4,512,512]{2,1,0:T(8,128)} %get-tuple-element.104, f32[512]{0:T(512)S(1)} %fusion.124, f32[4,512]{1,0:T(4,128)S(1)} %get-tuple-element.58, ...), kind=kLoop, calls=%fused_computation.66 | loop fusion | flops 14667776 | bytes 8462336 | tf_op jit(solution)/shard_map/reduce_sum | solution.py:76
  608.2 6.8 %multiply_reduce_fusion.21 = (f32[4,512]{1,0:T(4,128)S(1)}, f32[4,512]{1,0:T(4,128)S(1)}, f32[4,512]{1,0:T(4,128)S(1)}, f32[4,512]{1,0:T(4,128)S(1)}, f32[4,512]{1,0:T(4,128)S(1)}, /*index=5*/f32[4,512]{1,0:T(4,128)S(1)}) fusion(f32[4,512,512]{2,1,0:T(8,128)} %get-tuple-element.108, f32[512]{0:T(512)S(1)} %fusion.132, f32[4,512]{1,0:T(4,128)S(1)} %get-tuple-element.60, ...), kind=kLoop, calls=%fused_computation.68 | loop fusion | flops 14667776 | bytes 8462336 | tf_op jit(solution)/shard_map/reduce_sum | solution.py:76
  615.1 7.0 %multiply_reduce_fusion.23 = (f32[4,512]{1,0:T(4,128)S(1)}, f32[4,512]{1,0:T(4,128)S(1)}, f32[4,512]{1,0:T(4,128)S(1)}, f32[4,512]{1,0:T(4,128)S(1)}, f32[4,512]{1,0:T(4,128)S(1)}, /*index=5*/f32[4,512]{1,0:T(4,128)S(1)}) fusion(f32[4,512,512]{2,1,0:T(8,128)} %get-tuple-element.112, f32[512]{0:T(512)S(1)} %fusion.140, f32[4,512]{1,0:T(4,128)S(1)} %get-tuple-element.62, ...), kind=kLoop, calls=%fused_computation.70 | loop fusion | flops 14667776 | bytes 8462336 | tf_op jit(solution)/shard_map/reduce_sum | solution.py:76
  622.3 6.8 %multiply_reduce_fusion.25 = (f32[4,512]{1,0:T(4,128)S(1)}, f32[4,512]{1,0:T(4,128)S(1)}, f32[4,512]{1,0:T(4,128)S(1)}, f32[4,512]{1,0:T(4,128)S(1)}, f32[4,512]{1,0:T(4,128)S(1)}, /*index=5*/f32[4,512]{1,0:T(4,128)S(1)}) fusion(f32[4,512,512]{2,1,0:T(8,128)} %get-tuple-element.116, f32[512]{0:T(512)S(1)} %fusion.148, f32[4,512]{1,0:T(4,128)S(1)} %get-tuple-element.64, ...), kind=kLoop, calls=%fused_computation.72 | loop fusion | flops 14667776 | bytes 8462336 | tf_op jit(solution)/shard_map/reduce_sum | solution.py:76
  629.3 6.8 %multiply_reduce_fusion.27 = (f32[4,512]{1,0:T(4,128)S(1)}, f32[4,512]{1,0:T(4,128)S(1)}, f32[4,512]{1,0:T(4,128)S(1)}, f32[4,512]{1,0:T(4,128)S(1)}, f32[4,512]{1,0:T(4,128)S(1)}, /*index=5*/f32[4,512]{1,0:T(4,128)S(1)}) fusion(f32[4,512,512]{2,1,0:T(8,128)} %get-tuple-element.120, f32[512]{0:T(512)S(1)} %fusion.156, f32[4,512]{1,0:T(4,128)S(1)} %get-tuple-element.66, ...), kind=kLoop, calls=%fused_computation.74 | loop fusion | flops 14667776 | bytes 8462336 | tf_op jit(solution)/shard_map/reduce_sum | solution.py:76
  636.2 3.8 multiply_reduce_fusion.29
  (151 shorter events, 44.0 us)
Async XLA Ops:
  0.6 537.9 %copy-start = (bf16[32,16,256]{2,1,0:T(8,128)(2,1)S(1)}, bf16[32,16,256]{2,1,0:T(8,128)(2,1)}, u32[]{:S(2)}) copy-start(bf16[32,16,256]{2,1,0:T(8,128)(2,1)} %param.7) | copy-start | bytes 786436
  2.1 10.9 %all-to-all-start.3 = ((s32[16,4,8]{2,1,0:T(4,128)}), s32[16,4,8]{2,1,0:T(4,128)S(1)}, u32[]{:S(2)}, u32[]{:S(2)}) async-start(s32[16,4,8]{2,1,0:T(4,128)} %bitcast.28), calls=%async_computation.3 | async-start | bytes 65536 | tf_op jit(solution)/shard_map/all_to_all | solution.py:89
  13.0 15.5 %all-to-all-start.1 = ((s32[16,4,8]{2,1,0:T(4,128)}), s32[16,4,8]{2,1,0:T(4,128)S(1)}, u32[]{:S(2)}, u32[]{:S(2)}) async-start(s32[16,4,8]{2,1,0:T(4,128)} %bitcast.25), calls=%async_computation.1 | async-start | bytes 65536 | tf_op jit(solution)/shard_map/all_to_all | solution.py:90
  28.5 98.7 %copy-start.1 = (bf16[4,510,256]{2,0,1:T(4,128)(2,1)S(1)}, bf16[4,510,256]{2,0,1:T(4,128)(2,1)}, u32[]{:S(2)}) copy-start(bf16[4,510,256]{2,0,1:T(4,128)(2,1)} %param.8) | copy-start | bytes 3133444
  134.9 9.3 %copy-start.2 = (s32[2,64,2]{1,2,0:T(2,128)S(1)}, s32[2,64,2]{1,2,0:T(2,128)}, u32[]{:S(2)}) copy-start(s32[2,64,2]{1,2,0:T(2,128)} %param.11) | copy-start | bytes 3076
  134.9 10.9 %copy-start.3 = (bf16[2,128]{1,0:T(2,128)(2,1)S(1)}, bf16[2,128]{1,0:T(2,128)(2,1)}, u32[]{:S(2)}) copy-start(bf16[2,128]{1,0:T(2,128)(2,1)} %param.9) | copy-start | bytes 1540
  134.9 391.7 %all-to-all-start = ((bf16[16,4,510,256]{3,1,2,0:T(4,128)(2,1)}), bf16[16,4,510,256]{3,1,2,0:T(4,128)(2,1)}, u32[]{:S(2)}, u32[]{:S(2)}) async-start(bf16[16,4,510,256]{3,1,2,0:T(4,128)(2,1)} %stack.6), calls=%async_computation | async-start | bytes 33423360 | tf_op jit(solution)/shard_map/all_to_all | solution.py:56
